TPU v7x, 256 devices: a whole 4x4x8 slice. The times are simulated.
256 devices in a mesh: ctx: 32 (over y, x, core), head: 8 (over z).
Axes of the slice: x: 4, y: 4, z: 8, core: 2. Of those that a mesh axis runs over, the one named last changes fastest.
Arguments:
- tokens: bfloat16 [8192, 4096], P('ctx', 'head'), may hold values from -6 to 6
- policy_weight: bfloat16 [3, 4096, 2048], P(None, 'ctx', 'head'), may hold values from -0.09375 to 0.09375
- reference_weight: bfloat16 [3, 4096, 2048], P(None, 'ctx', 'head'), may hold values from -0.09375 to 0.09375
Outputs:
- difference: float32 [8192, 2048], P('ctx', 'head')
- input_grad: float32 [8192, 4096], P('ctx', 'head')
All inputs are finite; a program needn't handle non-finite values.
Results may differ from a plain program's by a relative error of at most 0.0027.
Values may be sent and summed in bfloat16 or wider, within the bound.
A program may use at most 64 MiB of HBM per device.

v0:
```python
import math
import jax
import jax.numpy as jnp
from jax import lax
from jax.sharding import PartitionSpec as P

HD = 128
HIGH = lax.Precision.HIGHEST


def prefix(value, axis, join, neutral, backward):
    count, mine = (lax.axis_size(axis), lax.axis_index(axis))
    pieces = jax.tree.map(lambda part: lax.all_gather(part, axis), value)
    if backward:
        pieces = jax.tree.map(lambda part: part[::-1], pieces)
        mine = count - 1 - mine
    total = jax.tree.map(
        lambda part, zero: jnp.full_like(part, 0) + jnp.asarray(zero, part.dtype), value, neutral
    )

    def hop(position, total):
        longer = join(total, jax.tree.map(lambda part: part[position], pieces))
        return jax.tree.map(lambda new, old: jnp.where(position < mine, new, old), longer, total)

    return lax.fori_loop(0, count - 1, hop, total)


def per_device(tokens, policy_weight, reference_weight):
    row_count = tokens.shape[0]
    local_width = policy_weight.shape[2]
    heads_here = local_width // HD
    seq_tokens = row_count * lax.axis_size("ctx")
    out_scale = 1.0 / math.sqrt(HD * seq_tokens)
    whole = lax.all_gather(tokens, "head", axis=1, tiled=True)
    policy_whole = lax.all_gather(policy_weight, "ctx", axis=1, tiled=True)
    qkv_pol = jnp.einsum("td,cdj->tcj", whole, policy_whole, preferred_element_type=jnp.float32)
    qkv_ref = jnp.einsum(
        "tn,cnj->tcj",
        whole,
        lax.all_gather(reference_weight, "ctx", axis=1, tiled=True),
        preferred_element_type=jnp.float32,
    )

    def split_heads(qkv):
        return [qkv[:, slot].reshape(row_count, heads_here, HD) for slot in range(3)]

    query_pol, key_pol, value_pol = split_heads(qkv_pol)
    query_ref, key_ref, value_ref = split_heads(qkv_ref)
    causal = jnp.tril(jnp.ones((row_count, row_count), jnp.float32))

    def inner(query, keys, values):
        scores = jnp.einsum("thd,shd->hts", query, keys, precision=HIGH) * causal
        return (scores, jnp.einsum("hts,shd->thd", scores, values, precision=HIGH))

    scores_pol, local_pol = inner(query_pol, key_pol, value_pol)
    _, local_ref = inner(query_ref, key_ref, value_ref)
    own_pol = jnp.einsum("thd,the->hde", key_pol, value_pol, precision=HIGH)
    own_ref = jnp.einsum("thd,the->hde", key_ref, value_ref, precision=HIGH)
    zeros = jnp.zeros((heads_here, HD, HD), jnp.float32)

    def add_pair(earlier, later):
        return (earlier[0] + later[0], earlier[1] + later[1])

    prefix_pol, prefix_ref = prefix((own_pol, own_ref), "ctx", add_pair, (zeros, zeros), False)
    out_pol = out_scale * (
        local_pol + jnp.einsum("thd,hde->the", query_pol, prefix_pol, precision=HIGH)
    )
    out_ref = out_scale * (
        local_ref + jnp.einsum("thd,hde->the", query_ref, prefix_ref, precision=HIGH)
    )
    difference = out_pol - out_ref
    weighted = jnp.einsum("thd,shd->hts", difference, value_pol, precision=HIGH) * causal
    grad_query = jnp.einsum("hts,shd->thd", weighted, key_pol, precision=HIGH)
    grad_query = out_scale * (
        grad_query + jnp.einsum("the,hde->thd", difference, prefix_pol, precision=HIGH)
    )
    later_own = jnp.einsum("thd,the->hde", query_pol, difference, precision=HIGH)
    suffix = prefix(later_own, "ctx", lambda earlier, later: earlier + later, zeros, True)
    grad_key = jnp.einsum("hts,thd->shd", weighted, query_pol, precision=HIGH)
    grad_key = out_scale * (
        grad_key + jnp.einsum("hde,she->shd", suffix, value_pol, precision=HIGH)
    )
    grad_value = jnp.einsum("hts,the->she", scores_pol, difference, precision=HIGH)
    grad_value = out_scale * (
        grad_value + jnp.einsum("hde,shd->she", suffix, key_pol, precision=HIGH)
    )
    grad_qkv = (
        jnp.stack([grad_query, grad_key, grad_value], 1)
        .reshape(row_count, 3, local_width)
        .astype(jnp.bfloat16)
    )
    partial_grad = jnp.einsum(
        "tcj,cdj->td", grad_qkv, policy_whole, preferred_element_type=jnp.float32
    )
    input_grad = lax.psum_scatter(partial_grad, "head", scatter_dimension=1, tiled=True)
    return (difference.reshape(row_count, local_width), input_grad)


def solution(mesh):
    in_specs = (P("ctx", "head"), P(None, "ctx", "head"), P(None, "ctx", "head"))
    out_specs = (P("ctx", "head"), P("ctx", "head"))
    return jax.shard_map(
        per_device, mesh=mesh, in_specs=in_specs, out_specs=out_specs, check_vma=False
    )
```

profile of v0, /device:TPU:1, one launch (start us, length us, event | category | flops | bytes accessed | tf_op | source)
XLA Modules:
  0.0 476.0 jit_solution(5663304150087823383)
XLA Ops:
  7.9 1.7 copy.27
  9.8 1.7 copy.31
  11.6 39.5 %all-gather.10.cloned.1.call-done = bf16[256,4096]{1,0:T(8,128)(2,1)} async-done(((bf16[256,512]{1,0:T(8,128)(2,1)}), bf16[256,4096]{1,0:T(8,128)(2,1)}) %all-gather.10.cloned.1.call-update) | async-done | bytes 2097168 | tf_op jit(solution)/shard_map/all_gather | solution.py:34
  51.0 65.1 %all-gather.12.cloned.1.call-done = bf16[3,4096,256]{1,2,0:T(8,128)(2,1)} async-done(((bf16[3,128,256]{1,2,0:T(8,128)(2,1)}), bf16[3,4096,256]{1,2,0:T(8,128)(2,1)}) %all-gather.12.cloned.1.call-update) | async-done | bytes 6291472 | tf_op jit(solution)/shard_map/all_gather | solution.py:35
  116.2 5.2 %fusion.2 = f32[256,3,256]{0,2,1:T(8,128)S(1)} fusion(bf16[3,4096,256]{1,2,0:T(8,128)(2,1)} %all-gather.12.cloned.1.call-done, bf16[256,4096]{1,0:T(8,128)(2,1)} %all-gather.10.cloned.1.call-done), kind=kOutput, calls=%fused_computation.6 | convolution fusion | flops 1610612736 | bytes 9175040 | tf_op jit(solution)/shard_map/td,cdj->tcj/dot_general | solution.py:36
  122.6 55.7 %all-gather.14.cloned.1.call-done = bf16[3,4096,256]{1,2,0:T(8,128)(2,1)} async-done(((bf16[3,128,256]{1,2,0:T(8,128)(2,1)}), bf16[3,4096,256]{1,2,0:T(8,128)(2,1)}) %all-gather.14.cloned.1.call-update) | async-done | bytes 6291472 | tf_op jit(solution)/shard_map/all_gather | solution.py:40
  178.3 5.2 %fusion = f32[256,3,256]{0,2,1:T(8,128)S(1)} fusion(bf16[3,4096,256]{1,2,0:T(8,128)(2,1)} %all-gather.14.cloned.1.call-done, bf16[256,4096]{1,0:T(8,128)(2,1)} %all-gather.10.cloned.1.call-done), kind=kOutput, calls=%fused_computation.4 | convolution fusion | flops 1610612736 | bytes 9175040 | tf_op jit(solution)/shard_map/tn,cnj->tcj/dot_general | solution.py:37
  187.4 44.7 %all-gather.16.cloned.1.call-done = f32[64,128,128]{2,1,0:T(8,128)} async-done(((f32[2,128,128]{2,1,0:T(8,128)}), f32[64,128,128]{2,1,0:T(8,128)}) %all-gather.16.cloned.1.call-update) | async-done | bytes 4194320 | tf_op jit(solution)/shard_map/all_gather | solution.py:13
  232.1 53.5 %all-gather.18.cloned.1.call-done = f32[64,128,128]{2,1,0:T(8,128)} async-done(((f32[2,128,128]{2,1,0:T(8,128)}), f32[64,128,128]{2,1,0:T(8,128)}) %all-gather.18.cloned.1.call-update) | async-done | bytes 4194320 | tf_op jit(solution)/shard_map/all_gather | solution.py:13
  285.6 33.7 %while.30 = (s32[]{:T(128)}, f32[2,128,128]{2,1,0:T(8,128)S(1)}, f32[2,128,128]{2,1,0:T(8,128)S(1)}, s32[]{:T(128)}, f32[32,2,128,128]{3,2,1,0:T(8,128)}, /*index=5*/f32[32,2,128,128]{3,2,1,0:T(8,128)}, s32[]{:T(128)}, s32[]{:T(128)}) while((s32[]{:T(128)}, f32[2,128,128]{2,1,0:T(8,128)S(1)}, f32[2,128,128]{2,1,0:T(8,128)S(1)}, ...), condition=%wide.region_1.2_spmd.clone, body=%wide.region_0.1_spmd.clone.sunk | while | flops 196612 | bytes 786549 | solution.py:25
  286.7 1.1 add_select_fusion.5
  287.8 1.1 add_select_fusion.5
  288.9 1.1 add_select_fusion.5
  290.0 1.1 add_select_fusion.5
  291.0 1.1 add_select_fusion.5
  292.1 1.1 add_select_fusion.5
  293.2 1.1 add_select_fusion.5
  294.3 1.1 add_select_fusion.5
  295.4 1.1 add_select_fusion.5
  296.5 1.1 add_select_fusion.5
  297.6 1.1 add_select_fusion.5
  298.7 1.1 add_select_fusion.5
  299.8 1.1 add_select_fusion.5
  304.1 1.1 add_select_fusion.5
  305.2 1.1 add_select_fusion.5
  306.3 1.1 add_select_fusion.5
  307.4 1.1 add_select_fusion.5
  324.2 47.8 %all-gather.20.cloned.1.call-done = f32[64,128,128]{2,1,0:T(8,128)} async-done(((f32[2,128,128]{2,1,0:T(8,128)}), f32[64,128,128]{2,1,0:T(8,128)}) %all-gather.20.cloned.1.call-update) | async-done | bytes 4194320 | tf_op jit(solution)/shard_map/all_gather | solution.py:13
  372.0 4.8 %rev.3 = f32[32,2,128,128]{3,2,1,0:T(8,128)} reverse(f32[32,2,128,128]{3,2,1,0:T(8,128)} %bitcast.106), dimensions={0} | reverse | bytes 8388608 | tf_op jit(solution)/shard_map/rev | solution.py:15
  376.8 30.1 %while.31 = (s32[]{:T(128)}, f32[2,128,128]{2,1,0:T(8,128)S(1)}, s32[]{:T(128)}, f32[32,2,128,128]{3,2,1,0:T(8,128)}, s32[]{:T(128)}, /*index=5*/s32[]{:T(128)}) while((s32[]{:T(128)}, f32[2,128,128]{2,1,0:T(8,128)S(1)}, s32[]{:T(128)}, f32[32,2,128,128]{3,2,1,0:T(8,128)}, s32[]{:T(128)}, /*index=5*/s32[]{:T(128)}) %tuple.75), condition=%wide.region_3.4_spmd.clone, body=%wide.region_2.3_spmd.clone.sunk | while | flops 98308 | bytes 393317 | solution.py:25
  407.9 6.6 %convolution_bitcast_fusion = f32[256,4096]{1,0:T(8,128)} fusion(bf16[3,4096,256]{1,2,0:T(8,128)(2,1)} %all-gather.12.cloned.1.call-done, bf16[256,1,256]{2,0,1:T(8,128)(2,1)S(1)} %copy.46, bf16[256,1,256]{2,0,1:T(8,128)(2,1)S(1)} %copy.45, bf16[256,1,256]{2,0,1:T(8,128)(2,1)S(1)} %copy.44), kind=kOutput, calls=%fused_computation.3 | convolution fusion | flops 1611005952 | bytes 10878976 | tf_op jit(solution)/shard_map/tcj,cdj->td/dot_general | solution.py:92
  415.5 53.7 %reduce-scatter.2.cloned.1.call-done = f32[256,512]{1,0:T(8,128)} async-done(((f32[256,4096]{1,0:T(8,128)}), f32[256,512]{1,0:T(8,128)}) %reduce-scatter.2.cloned.1.call-update) | async-done | bytes 524304 | tf_op jit(solution)/shard_map/reduce_scatter | solution.py:95
  (85 shorter events, 56.8 us)
Async XLA Ops:
  7.2 43.9 %all-gather.10.cloned.1.call-start = ((), (), s32[]{:S(2)}) async-start(), calls=%async_computation.1 | async-start | bytes 2359296 | tf_op jit(solution)/shard_map/all_gather | solution.py:34
  7.9 108.3 %all-gather.12.cloned.1.call-start = ((), (), s32[]{:S(2)}) async-start(), calls=%async_computation.2 | async-start | bytes 6488064 | tf_op jit(solution)/shard_map/all_gather | solution.py:35
  9.7 168.6 %all-gather.14.cloned.1.call-start = ((), (), s32[]{:S(2)}) async-start(), calls=%async_computation.3 | async-start | bytes 6488064 | tf_op jit(solution)/shard_map/all_gather | solution.py:40
  11.5 220.6 %all-gather.16.cloned.1.call-start = ((), (), s32[]{:S(2)}) async-start(), calls=%async_computation.5 | async-start | bytes 4325376 | tf_op jit(solution)/shard_map/all_gather | solution.py:13
  122.5 163.1 %all-gather.18.cloned.1.call-start = ((), (), s32[]{:S(2)}) async-start(), calls=%async_computation.6 | async-start | bytes 4325376 | tf_op jit(solution)/shard_map/all_gather | solution.py:13
  184.7 187.3 %all-gather.20.cloned.1.call-start = ((), (), s32[]{:S(2)}) async-start(), calls=%async_computation.7 | async-start | bytes 4325376 | tf_op jit(solution)/shard_map/all_gather | solution.py:13
  321.3 147.8 %reduce-scatter.2.cloned.1.call-start = ((), (), s32[]{:S(2)}) async-start(), calls=%async_computation.4 | async-start | bytes 4718592 | tf_op jit(solution)/shard_map/reduce_scatter | solution.py:95
Sparse Core Ops, SparseCore 0:
  9.8 41.2 all-gather.9
  54.1 62.0 all-gather.11
  119.2 59.0 all-gather.13
  181.3 50.7 all-gather.15
  235.1 50.5 all-gather.17
  321.4 50.5 all-gather.19
  414.7 54.3 reduce-scatter.1
where the time goes:
time: 477 us; the launch traced here: 476 us
  waiting for transfers between devices  361 us (76%)
  other arithmetic  62.5 us (13%)
  matrix products  27 us (6%)
  between operations  14.3 us (3%)
  local copies, waits for them, and re-layouts  9.49 us (2%)
    all_gather x3, waiting for transfers between devices, prefix(): pieces = jax.tree.map(lambda part: lax.all_gather(part, axis), value)  146 us
    all_gather x1, waiting for transfers between devices, per_device(): policy_whole = lax.all_gather(policy_weight, 'ctx', axis=1, tiled=True)  65.1 us
    select_n x62, other arithmetic, hop(): jnp.where(position < mine, new, old)  62.4 us
    all_gather x1, waiting for transfers between devices, per_device(): lax.all_gather(reference_weight, 'ctx', axis=1, tiled=True)  55.7 us
    reduce_scatter x1, waiting for transfers between devices, per_device(): lax.psum_scatter(partial_grad, 'head', scatter_dimension=1, tiled=True)  53.7 us
    all_gather x1, waiting for transfers between devices, per_device(): whole = lax.all_gather(tokens, 'head', axis=1, tiled=True)  39.5 us
  transfers between devices with their start and end apart: 7, of which 7 were waited for; matrix products, arithmetic and copies ran while one was open for 5% of the time, Pallas kernels for 0%

commit v1 on v0

--- a/solution.py
+++ b/solution.py
@@ -31,7 +31,12 @@
     heads_here = local_width // HD
     seq_tokens = row_count * lax.axis_size("ctx")
     out_scale = 1.0 / math.sqrt(HD * seq_tokens)
-    whole = lax.all_gather(tokens, "head", axis=1, tiled=True)
+    ring = [tokens]
+    for hop_ in range(7):
+        ring.append(lax.ppermute(ring[-1], "head", [(dev, (dev + 1) % 8) for dev in range(8)]))
+    whole = jnp.roll(
+        jnp.concatenate(ring[::-1], axis=1), (lax.axis_index("head") + 1) * ring[0].shape[1], axis=1
+    )
     policy_whole = lax.all_gather(policy_weight, "ctx", axis=1, tiled=True)
     qkv_pol = jnp.einsum("td,cdj->tcj", whole, policy_whole, preferred_element_type=jnp.float32)
     qkv_ref = jnp.einsum(

time: 477 us -> 436 us (0.914)
  waiting for transfers between devices: 361 us -> 305 us
  local copies, waits for them, and re-layouts: 9.49 us -> 21.6 us
    all_gather x1, waiting for transfers between devices: 65.1 us -> 0.01 us  [per_device(): policy_whole = lax.all_gather(policy_weight, 'ctx', axis=1, tiled=True)]
    ppermute x0 -> x7, waiting for transfers between devices: none -> 53.7 us  [per_device(): lax.ppermute(ring[-1], 'head', [(dev, (dev + 1) % 8) for dev in range(8)])]
    all_gather x1 -> x0, waiting for transfers between devices: 39.5 us -> none  [per_device(): whole = lax.all_gather(tokens, 'head', axis=1, tiled=True)]
    unnamed x3 -> x20, local copies, waits for them, and re-layouts: 4.32 us -> 15.7 us
  transfers between devices with their start and end apart: 7 -> 13, of which waited for: 7 -> 12; matrix products, arithmetic and copies ran while one was open for 5% -> 7% of each run, Pallas kernels for 0% -> 0%
where the time goes in v1:
time: 436 us; the launch traced here: 435 us
  waiting for transfers between devices  305 us (70%)
  other arithmetic  62.5 us (14%)
  matrix products  27 us (6%)
  local copies, waits for them, and re-layouts  21.6 us (5%)
  between operations  14.3 us (3%)
    all_gather x3, waiting for transfers between devices, prefix(): pieces = jax.tree.map(lambda part: lax.all_gather(part, axis), value)  146 us
    select_n x62, other arithmetic, hop(): jnp.where(position < mine, new, old)  62.4 us
    ppermute x7, waiting for transfers between devices, per_device(): lax.ppermute(ring[-1], 'head', [(dev, (dev + 1) % 8) for dev in range(8)])  53.7 us
    reduce_scatter x1, waiting for transfers between devices, per_device(): lax.psum_scatter(partial_grad, 'head', scatter_dimension=1, tiled=True)  53.7 us
    all_gather x1, waiting for transfers between devices, per_device(): lax.all_gather(reference_weight, 'ctx', axis=1, tiled=True)  51.1 us
    unnamed x20, local copies, waits for them, and re-layouts  15.7 us
  transfers between devices with their start and end apart: 13, of which 12 were waited for; matrix products, arithmetic and copies ran while one was open for 7% of the time, Pallas kernels for 0%

profile of v1, /device:TPU:1, one launch (start us, length us, event | category | flops | bytes accessed | tf_op | source)
XLA Modules:
  0.0 434.6 jit_solution(12237844233754317115)
XLA Ops:
  7.2 1.8 copy.27
  9.1 1.7 copy.31
  10.9 2.5 collective-permute-start
  13.4 10.2 %collective-permute-done = bf16[256,512]{1,0:T(8,128)(2,1)S(1)} collective-permute-done((bf16[256,512]{1,0:T(8,128)(2,1)}, bf16[256,512]{1,0:T(8,128)(2,1)S(1)}, u32[]{:S(2)}, u32[]{:S(2)}) %collective-permute-start) | collective-permute-done | bytes 262176 | tf_op jit(solution)/shard_map/ppermute | solution.py:36
  23.6 7.8 %collective-permute-done.1 = bf16[256,512]{1,0:T(8,128)(2,1)S(1)} collective-permute-done((bf16[256,512]{1,0:T(8,128)(2,1)S(1)}, bf16[256,512]{1,0:T(8,128)(2,1)S(1)}, u32[]{:S(2)}, u32[]{:S(2)}) %collective-permute-start.1) | collective-permute-done | bytes 262176 | tf_op jit(solution)/shard_map/ppermute | solution.py:36
  31.4 6.9 %collective-permute-done.2 = bf16[256,512]{1,0:T(8,128)(2,1)S(1)} collective-permute-done((bf16[256,512]{1,0:T(8,128)(2,1)S(1)}, bf16[256,512]{1,0:T(8,128)(2,1)S(1)}, u32[]{:S(2)}, u32[]{:S(2)}) %collective-permute-start.2) | collective-permute-done | bytes 262176 | tf_op jit(solution)/shard_map/ppermute | solution.py:36
  38.3 6.4 %collective-permute-done.3 = bf16[256,512]{1,0:T(8,128)(2,1)S(1)} collective-permute-done((bf16[256,512]{1,0:T(8,128)(2,1)S(1)}, bf16[256,512]{1,0:T(8,128)(2,1)S(1)}, u32[]{:S(2)}, u32[]{:S(2)}) %collective-permute-start.3) | collective-permute-done | bytes 262176 | tf_op jit(solution)/shard_map/ppermute | solution.py:36
  44.7 6.4 %collective-permute-done.4 = bf16[256,512]{1,0:T(8,128)(2,1)S(1)} collective-permute-done((bf16[256,512]{1,0:T(8,128)(2,1)S(1)}, bf16[256,512]{1,0:T(8,128)(2,1)S(1)}, u32[]{:S(2)}, u32[]{:S(2)}) %collective-permute-start.4) | collective-permute-done | bytes 262176 | tf_op jit(solution)/shard_map/ppermute | solution.py:36
  51.1 7.7 %collective-permute-done.5 = bf16[256,512]{1,0:T(8,128)(2,1)S(1)} collective-permute-done((bf16[256,512]{1,0:T(8,128)(2,1)S(1)}, bf16[256,512]{1,0:T(8,128)(2,1)S(1)}, u32[]{:S(2)}, u32[]{:S(2)}) %collective-permute-start.5) | collective-permute-done | bytes 262176 | tf_op jit(solution)/shard_map/ppermute | solution.py:36
  58.8 8.3 %collective-permute-done.6 = bf16[256,512]{1,0:T(8,128)(2,1)S(1)} collective-permute-done((bf16[256,512]{1,0:T(8,128)(2,1)S(1)}, bf16[256,512]{1,0:T(8,128)(2,1)S(1)}, u32[]{:S(2)}, u32[]{:S(2)}) %collective-permute-start.6) | collective-permute-done | bytes 262176 | tf_op jit(solution)/shard_map/ppermute | solution.py:36
  79.3 5.2 %fusion.2 = f32[256,3,256]{0,2,1:T(8,128)S(1)} fusion(bf16[3,4096,256]{1,2,0:T(8,128)(2,1)} %all-gather.9.cloned.1.call-done, bf16[256,8192]{1,0:T(8,128)(2,1)} %constant_dynamic-update-slice_fusion, s32[]{:T(128)S(6)} %select_n.75), kind=kOutput, calls=%fused_computation.6 | convolution fusion | flops 1610612736 | bytes 9175044 | tf_op jit(solution)/shard_map/td,cdj->tcj/dot_general | solution.py:41
  85.7 51.1 %all-gather.11.cloned.1.call-done = bf16[3,4096,256]{1,2,0:T(8,128)(2,1)} async-done(((bf16[3,128,256]{1,2,0:T(8,128)(2,1)}), bf16[3,4096,256]{1,2,0:T(8,128)(2,1)}) %all-gather.11.cloned.1.call-update) | async-done | bytes 6291472 | tf_op jit(solution)/shard_map/all_gather | solution.py:45
  136.8 5.2 %fusion = f32[256,3,256]{0,2,1:T(8,128)S(1)} fusion(bf16[3,4096,256]{1,2,0:T(8,128)(2,1)} %all-gather.11.cloned.1.call-done, bf16[256,8192]{1,0:T(8,128)(2,1)} %constant_dynamic-update-slice_fusion, s32[]{:T(128)S(6)} %select_n.75), kind=kOutput, calls=%fused_computation.4 | convolution fusion | flops 1610612736 | bytes 9175044 | tf_op jit(solution)/shard_map/tn,cnj->tcj/dot_general | solution.py:42
  146.0 44.7 %all-gather.13.cloned.1.call-done = f32[64,128,128]{2,1,0:T(8,128)} async-done(((f32[2,128,128]{2,1,0:T(8,128)}), f32[64,128,128]{2,1,0:T(8,128)}) %all-gather.13.cloned.1.call-update) | async-done | bytes 4194320 | tf_op jit(solution)/shard_map/all_gather | solution.py:13
  190.7 53.5 %all-gather.15.cloned.1.call-done = f32[64,128,128]{2,1,0:T(8,128)} async-done(((f32[2,128,128]{2,1,0:T(8,128)}), f32[64,128,128]{2,1,0:T(8,128)}) %all-gather.15.cloned.1.call-update) | async-done | bytes 4194320 | tf_op jit(solution)/shard_map/all_gather | solution.py:13
  244.3 33.7 %while.30 = (s32[]{:T(128)}, f32[2,128,128]{2,1,0:T(8,128)S(1)}, f32[2,128,128]{2,1,0:T(8,128)S(1)}, s32[]{:T(128)}, f32[32,2,128,128]{3,2,1,0:T(8,128)}, /*index=5*/f32[32,2,128,128]{3,2,1,0:T(8,128)}, s32[]{:T(128)}, s32[]{:T(128)}) while((s32[]{:T(128)}, f32[2,128,128]{2,1,0:T(8,128)S(1)}, f32[2,128,128]{2,1,0:T(8,128)S(1)}, ...), condition=%wide.region_1.2_spmd.clone, body=%wide.region_0.1_spmd.clone.sunk | while | flops 196612 | bytes 786549 | solution.py:25
  246.4 1.1 add_select_fusion.5
  248.6 1.1 add_select_fusion.5
  249.7 1.1 add_select_fusion.5
  251.9 1.1 add_select_fusion.5
  254.1 1.1 add_select_fusion.5
  257.3 1.1 add_select_fusion.5
  259.5 1.1 add_select_fusion.5
  261.7 1.1 add_select_fusion.5
  262.8 1.1 add_select_fusion.5
  264.9 1.1 add_select_fusion.5
  267.1 1.1 add_select_fusion.5
  282.7 48.0 %all-gather.17.cloned.1.call-done = f32[64,128,128]{2,1,0:T(8,128)} async-done(((f32[2,128,128]{2,1,0:T(8,128)}), f32[64,128,128]{2,1,0:T(8,128)}) %all-gather.17.cloned.1.call-update) | async-done | bytes 4194320 | tf_op jit(solution)/shard_map/all_gather | solution.py:13
  330.6 4.7 %rev.3 = f32[32,2,128,128]{3,2,1,0:T(8,128)} reverse(f32[32,2,128,128]{3,2,1,0:T(8,128)} %bitcast.106), dimensions={0} | reverse | bytes 8388608 | tf_op jit(solution)/shard_map/rev | solution.py:15
  335.4 30.2 %while.31 = (s32[]{:T(128)}, f32[2,128,128]{2,1,0:T(8,128)S(1)}, s32[]{:T(128)}, f32[32,2,128,128]{3,2,1,0:T(8,128)}, s32[]{:T(128)}, /*index=5*/s32[]{:T(128)}) while((s32[]{:T(128)}, f32[2,128,128]{2,1,0:T(8,128)S(1)}, s32[]{:T(128)}, f32[32,2,128,128]{3,2,1,0:T(8,128)}, s32[]{:T(128)}, /*index=5*/s32[]{:T(128)}) %tuple.75), condition=%wide.region_3.4_spmd.clone, body=%wide.region_2.3_spmd.clone.sunk | while | flops 98308 | bytes 393317 | solution.py:25
  366.6 6.6 %convolution_bitcast_fusion = f32[256,4096]{1,0:T(8,128)} fusion(bf16[3,4096,256]{1,2,0:T(8,128)(2,1)} %all-gather.9.cloned.1.call-done, bf16[256,1,256]{2,0,1:T(8,128)(2,1)S(1)} %copy.46, bf16[256,1,256]{2,0,1:T(8,128)(2,1)S(1)} %copy.45, bf16[256,1,256]{2,0,1:T(8,128)(2,1)S(1)} %copy.44), kind=kOutput, calls=%fused_computation.3 | convolution fusion | flops 1611005952 | bytes 10878976 | tf_op jit(solution)/shard_map/tcj,cdj->td/dot_general | solution.py:97
  374.1 53.7 %reduce-scatter.2.cloned.1.call-done = f32[256,512]{1,0:T(8,128)} async-done(((f32[256,4096]{1,0:T(8,128)}), f32[256,512]{1,0:T(8,128)}) %reduce-scatter.2.cloned.1.call-update) | async-done | bytes 524304 | tf_op jit(solution)/shard_map/reduce_scatter | solution.py:100
  (114 shorter events, 74.5 us)
Async XLA Ops:
  7.2 65.2 %copy-start = (bf16[256,512]{1,0:T(8,128)(2,1)S(1)}, bf16[256,512]{1,0:T(8,128)(2,1)}, u32[]{:S(2)}) copy-start(bf16[256,512]{1,0:T(8,128)(2,1)} %param.7) | copy-start | bytes 786436
  7.2 72.1 %all-gather.9.cloned.1.call-start = ((), (), s32[]{:S(2)}) async-start(), calls=%async_computation.1 | async-start | bytes 6488064 | tf_op jit(solution)/shard_map/all_gather | solution.py:40
  9.0 127.8 %all-gather.11.cloned.1.call-start = ((), (), s32[]{:S(2)}) async-start(), calls=%async_computation.2 | async-start | bytes 6488064 | tf_op jit(solution)/shard_map/all_gather | solution.py:45
  10.8 179.9 %all-gather.13.cloned.1.call-start = ((), (), s32[]{:S(2)}) async-start(), calls=%async_computation.4 | async-start | bytes 4325376 | tf_op jit(solution)/shard_map/all_gather | solution.py:13
  10.9 12.7 %collective-permute-start = (bf16[256,512]{1,0:T(8,128)(2,1)}, bf16[256,512]{1,0:T(8,128)(2,1)S(1)}, u32[]{:S(2)}, u32[]{:S(2)}) collective-permute-start(bf16[256,512]{1,0:T(8,128)(2,1)} %param.7), channel_id=1, source_target_pairs={{0,1},{1,2},{2,3},{3,4},{4,5},{5,6},{6,7},{7,0},{8,9},{9,10},{10,1... | collective-permute-start | bytes 786440 | tf_op jit(solution)/shard_map/ppermute | solution.py:36
  23.6 7.8 %collective-permute-start.1 = (bf16[256,512]{1,0:T(8,128)(2,1)S(1)}, bf16[256,512]{1,0:T(8,128)(2,1)S(1)}, u32[]{:S(2)}, u32[]{:S(2)}) collective-permute-start(bf16[256,512]{1,0:T(8,128)(2,1)S(1)} %collective-permute-done), channel_id=1, source_target_pairs={{0,1},{1,2},{2,3},{3,4},{4,5},{5,6},{6,7},{7,0},{8,9},{9,10},{10,1... | collective-permute-start | bytes 786440 | tf_op jit(solution)/shard_map/ppermute | solution.py:36
  31.4 6.9 %collective-permute-start.2 = (bf16[256,512]{1,0:T(8,128)(2,1)S(1)}, bf16[256,512]{1,0:T(8,128)(2,1)S(1)}, u32[]{:S(2)}, u32[]{:S(2)}) collective-permute-start(bf16[256,512]{1,0:T(8,128)(2,1)S(1)} %collective-permute-done.1), channel_id=1, source_target_pairs={{0,1},{1,2},{2,3},{3,4},{4,5},{5,6},{6,7},{7,0},{8,9},{9,10},{10,1... | collective-permute-start | bytes 786440 | tf_op jit(solution)/shard_map/ppermute | solution.py:36
  38.3 6.4 %collective-permute-start.3 = (bf16[256,512]{1,0:T(8,128)(2,1)S(1)}, bf16[256,512]{1,0:T(8,128)(2,1)S(1)}, u32[]{:S(2)}, u32[]{:S(2)}) collective-permute-start(bf16[256,512]{1,0:T(8,128)(2,1)S(1)} %collective-permute-done.2), channel_id=1, source_target_pairs={{0,1},{1,2},{2,3},{3,4},{4,5},{5,6},{6,7},{7,0},{8,9},{9,10},{10,1... | collective-permute-start | bytes 786440 | tf_op jit(solution)/shard_map/ppermute | solution.py:36
  44.7 6.4 %collective-permute-start.4 = (bf16[256,512]{1,0:T(8,128)(2,1)S(1)}, bf16[256,512]{1,0:T(8,128)(2,1)S(1)}, u32[]{:S(2)}, u32[]{:S(2)}) collective-permute-start(bf16[256,512]{1,0:T(8,128)(2,1)S(1)} %collective-permute-done.3), channel_id=1, source_target_pairs={{0,1},{1,2},{2,3},{3,4},{4,5},{5,6},{6,7},{7,0},{8,9},{9,10},{10,1... | collective-permute-start | bytes 786440 | tf_op jit(solution)/shard_map/ppermute | solution.py:36
  51.1 7.7 %collective-permute-start.5 = (bf16[256,512]{1,0:T(8,128)(2,1)S(1)}, bf16[256,512]{1,0:T(8,128)(2,1)S(1)}, u32[]{:S(2)}, u32[]{:S(2)}) collective-permute-start(bf16[256,512]{1,0:T(8,128)(2,1)S(1)} %collective-permute-done.4), channel_id=1, source_target_pairs={{0,1},{1,2},{2,3},{3,4},{4,5},{5,6},{6,7},{7,0},{8,9},{9,10},{10,1... | collective-permute-start | bytes 786440 | tf_op jit(solution)/shard_map/ppermute | solution.py:36
  58.8 8.3 %collective-permute-start.6 = (bf16[256,512]{1,0:T(8,128)(2,1)S(1)}, bf16[256,512]{1,0:T(8,128)(2,1)S(1)}, u32[]{:S(2)}, u32[]{:S(2)}) collective-permute-start(bf16[256,512]{1,0:T(8,128)(2,1)S(1)} %collective-permute-done.5), channel_id=1, source_target_pairs={{0,1},{1,2},{2,3},{3,4},{4,5},{5,6},{6,7},{7,0},{8,9},{9,10},{10,1... | collective-permute-start | bytes 786440 | tf_op jit(solution)/shard_map/ppermute | solution.py:36
  85.6 158.6 %all-gather.15.cloned.1.call-start = ((), (), s32[]{:S(2)}) async-start(), calls=%async_computation.5 | async-start | bytes 4325376 | tf_op jit(solution)/shard_map/all_gather | solution.py:13
  143.2 187.4 %all-gather.17.cloned.1.call-start = ((), (), s32[]{:S(2)}) async-start(), calls=%async_computation.6 | async-start | bytes 4325376 | tf_op jit(solution)/shard_map/all_gather | solution.py:13
  279.9 147.8 %reduce-scatter.2.cloned.1.call-start = ((), (), s32[]{:S(2)}) async-start(), calls=%async_computation.3 | async-start | bytes 4718592 | tf_op jit(solution)/shard_map/reduce_scatter | solution.py:100
Sparse Core Ops, SparseCore 0:
  11.1 63.5 all-gather.8
  77.7 59.0 all-gather.10
  139.9 50.7 all-gather.12
  193.7 50.5 all-gather.14
  280.1 50.5 all-gather.16
  373.4 54.3 reduce-scatter.1
